TPU v7x, 256 devices: a whole 4x4x8 slice. The times are simulated.
256 devices in a mesh: seq: 16 (over y, x), tp: 16 (over z, core).
Axes of the slice: x: 4, y: 4, z: 8, core: 2. Of those that a mesh axis runs over, the one named last changes fastest.
Arguments:
- block_in: bfloat16 [2048, 8192], P(None, 'seq'), may hold values from -6 to 6
- w_in: bfloat16 [3, 8192, 8192], P(None, 'seq', 'tp'), may hold values from -0.0625 to 0.0625
- filt: float32 [512, 128], P('tp'), may hold values from -0.5 to 0.5
- skip: float32 [8192], P('tp'), may hold values from -3 to 3
- grad_y: bfloat16 [2048, 8192], P('seq', 'tp'), may hold values from -6 to 6
Outputs:
- block_out: bfloat16 [2048, 8192], P('seq', 'tp')
- grad_x: bfloat16 [2048, 8192], P('tp', 'seq')
- grad_w: float32 [3, 8192, 8192], P(None, 'seq', 'tp')
- grad_filt: float32 [512, 128], P('tp')
- grad_skip: float32 [8192], P('tp')
All inputs are finite; a program needn't handle non-finite values.
Results may differ from a plain program's by a relative error of at most 0.025.
Values may be sent and summed in bfloat16 or wider, within the bound.
A program may use at most 128 MiB of HBM per device.

v0:
```python
import jax
import jax.numpy as jnp
from jax import lax
from jax.sharding import PartitionSpec as P


def passed_along(array, axis, by):
    size = lax.axis_size(axis)
    pairs = [(i, i + by) for i in range(size) if 0 <= i + by < size]
    return lax.ppermute(array, axis, pairs)


def project_rows(block_in, weights):
    return jnp.einsum("tf,jfc->tjc", block_in, weights, preferred_element_type=jnp.float32)


def send_rim(u, slab, taps):
    return passed_along(u[slab - (taps - 1) :].astype(jnp.bfloat16), "seq", 1).astype(jnp.float32)


def toeplitz(row_taps, slab):
    groups_dev, taps = row_taps.shape
    width = slab + taps
    padded = jnp.concatenate([row_taps, jnp.zeros((groups_dev, slab), jnp.float32)], axis=1)
    tiled = jnp.tile(padded, (1, slab))[:, : slab * (width - 1)]
    return tiled.reshape(groups_dev, slab, width - 1)


def diagonal_sums(products, taps):
    groups_dev, slab, cols = products.shape
    width = cols + 1
    padded = jnp.concatenate([products, jnp.zeros((groups_dev, slab, 1), jnp.float32)], axis=2)
    flat = jnp.concatenate(
        [padded.reshape(groups_dev, slab * width), jnp.zeros((groups_dev, slab), jnp.float32)],
        axis=1,
    )
    skewed = flat.reshape(groups_dev, slab, width + 1)[:, :, :taps]
    return jnp.sum(skewed, axis=1)[:, ::-1]


def per_device(block_in, w_in, filt, skip, grad_y):
    n_seq = lax.axis_size("seq")
    slab = grad_y.shape[0]
    chans = w_in.shape[2]
    groups_dev = filt.shape[0]
    group_ch = chans // groups_dev
    taps = filt.shape[1]
    total_rows = slab * n_seq
    scale = total_rows ** (-0.5)
    highest = lax.Precision.HIGHEST
    sums = lax.psum_scatter(
        project_rows(block_in, w_in), "seq", scatter_dimension=0, tiled=True
    ).astype(jnp.bfloat16)
    gate = sums[:, 0].astype(jnp.float32)
    key = sums[:, 1].astype(jnp.float32)
    value = sums[:, 2].astype(jnp.float32)
    u = key * value
    prior = send_rim(u, slab, taps)
    extended = jnp.concatenate([prior, u], axis=0).reshape(slab + taps - 1, groups_dev, group_ch)
    causal_mat = toeplitz(filt[:, ::-1], slab)
    anti_mat = toeplitz(filt, slab)
    skip_row = skip[None, :]
    conv = jnp.einsum("gts,sgc->tgc", causal_mat, extended, precision=highest).reshape(slab, chans)
    z = conv + skip_row * u
    block_out = (gate * z).astype(jnp.bfloat16)
    grad_out = grad_y.astype(jnp.float32)
    d_gate = grad_out * z
    dz = grad_out * gate
    after = passed_along(dz[: taps - 1].astype(jnp.bfloat16), "seq", -1).astype(jnp.float32)
    extended_dz = jnp.concatenate([dz, after], axis=0).reshape(
        slab + taps - 1, groups_dev, group_ch
    )
    anti = jnp.einsum("gts,sgc->tgc", anti_mat, extended_dz, precision=highest).reshape(slab, chans)
    du = anti + skip_row * dz
    dz_groups = dz.reshape(slab, groups_dev, group_ch)
    products = jnp.einsum("tgc,sgc->gts", dz_groups, extended, precision=highest)
    filt_part = diagonal_sums(products, taps)
    skip_part = jnp.sum(dz * u, axis=0)
    filt_sum, skip_sum = lax.psum((filt_part, skip_part), "seq")
    grad_filt = filt_sum * scale
    grad_skip = skip_sum * scale
    grads_local = jnp.stack([d_gate, du * value, du * key], axis=1).astype(jnp.bfloat16)
    gathered = lax.all_gather(grads_local, "seq", axis=0, tiled=True)
    grad_x = lax.psum_scatter(
        jnp.einsum("tjc,jfc->tf", gathered, w_in, preferred_element_type=jnp.float32).astype(
            jnp.bfloat16
        ),
        "tp",
        scatter_dimension=0,
        tiled=True,
    )
    grad_w = (
        jnp.einsum("tf,tjc->jfc", block_in, gathered, preferred_element_type=jnp.float32) * scale
    )
    return (block_out, grad_x, grad_w, grad_filt, grad_skip)


def solution(mesh):
    in_specs = (P(None, "seq"), P(None, "seq", "tp"), P("tp", None), P("tp"), P("seq", "tp"))
    out_specs = (P("seq", "tp"), P("tp", "seq"), P(None, "seq", "tp"), P("tp", None), P("tp"))
    return jax.shard_map(
        per_device, mesh=mesh, in_specs=in_specs, out_specs=out_specs, check_vma=False
    )
```

profile of v0, /device:TPU:32, one launch (start us, length us, event | category | flops | bytes accessed | tf_op | source)
XLA Modules:
  0.0 363.3 jit_solution(6141584846466858381)
XLA Ops:
  7.2 1.5 copy-done
  8.8 7.7 %fusion.2 = f32[2048,3,512]{2,0,1:T(8,128)} fusion(bf16[3,512,512]{2,1,0:T(8,128)(2,1)} %param.6, bf16[2048,512]{1,0:T(8,128)(2,1)S(1)} %copy-done), kind=kOutput, calls=%fused_computation.5 | convolution fusion | flops 3221225472 | bytes 16252928 | tf_op jit(solution)/shard_map/tf,jfc->tjc/dot_general | solution.py:14
  16.6 102.1 %reduce-scatter.3.cloned.1.call-done = f32[128,3,512]{2,0,1:T(8,128)} async-done(((f32[2048,3,512]{2,0,1:T(8,128)}), f32[128,3,512]{2,0,1:T(8,128)}) %reduce-scatter.3.cloned.1.call-update) | async-done | bytes 786448 | tf_op jit(solution)/shard_map/reduce_scatter | solution.py:51
  121.7 2.4 copy.27
  124.2 2.2 slice.40
  126.4 9.4 %reshape.56 = f32[32,128,255]{2,1,0:T(8,128)} reshape(f32[32,32640]{1,0:T(8,128)} %slice.40) | data formatting | bytes 8355840 | tf_op jit(solution)/shard_map/reshape | solution.py:26
  136.1 2.4 copy.26
  138.6 2.2 slice.38
  140.8 9.4 %reshape.53 = f32[32,128,255]{2,1,0:T(8,128)} reshape(f32[32,32640]{1,0:T(8,128)} %slice.38) | data formatting | bytes 8355840 | tf_op jit(solution)/shard_map/reshape | solution.py:26
  150.9 5.2 %collective-permute-start = (bf16[127,512]{1,0:T(8,128)(2,1)}, bf16[127,512]{1,0:T(8,128)(2,1)}, u32[]{:S(2)}, u32[]{:S(2)}) collective-permute-start(bf16[127,512]{1,0:T(8,128)(2,1)} %slice.79), channel_id=1, source_target_pairs={{0,16},{16,32},{32,48},{48,64},{64,80},{80,96},{96,112},{112,128},... | collective-permute-start | bytes 390152 | tf_op jit(solution)/shard_map/ppermute | solution.py:10
  158.2 6.4 %fusion.14 = f32[32,16,128]{2,1,0:T(8,128)} fusion(f32[255,32,16]{0,2,1:T(8,128)S(1)} %bitcast.89, f32[32,128,255]{2,1,0:T(8,128)} %reshape.56), kind=kOutput, calls=%fused_computation.34 | convolution fusion | flops 200540160 | bytes 4962304 | tf_op jit(solution)/shard_map/gts,sgc->tgc/dot_general | solution.py:73
  164.6 1.8 copy.21
  169.4 5.2 %fusion.13 = f32[32,16,128]{2,1,0:T(8,128)S(1)} fusion(f32[255,32,16]{0,2,1:T(8,128)S(1)} %bitcast.87, f32[32,128,255]{2,1,0:T(8,128)} %reshape.53), kind=kOutput, calls=%fused_computation.33 | convolution fusion | flops 200540160 | bytes 4962304 | tf_op jit(solution)/shard_map/gts,sgc->tgc/dot_general | solution.py:63
  175.5 1.9 fusion.12
  178.2 66.9 %all-gather.2.cloned.1.call-done = bf16[2048,3,512]{2,0,1:T(8,128)(2,1)} async-done(((bf16[128,3,512]{2,0,1:T(8,128)(2,1)}), bf16[2048,3,512]{2,0,1:T(8,128)(2,1)}) %all-gather.2.cloned.1.call-update) | async-done | bytes 6291472 | tf_op jit(solution)/shard_map/all_gather | solution.py:83
  245.2 8.0 %bitcast_convert_fusion = bf16[2048,512]{1,0:T(8,128)(2,1)} fusion(bf16[2048,3,512]{2,0,1:T(8,128)(2,1)} %all-gather.2.cloned.1.call-done, bf16[3,512,512]{2,1,0:T(8,128)(2,1)} %param.6), kind=kOutput, calls=%fused_computation | convolution fusion | flops 3222274048 | bytes 9961472 | tf_op jit(solution)/shard_map/tjc,jfc->tf/dot_general | solution.py:85
  253.4 3.5 fusion.15
  257.3 2.4 copy.28
  259.7 2.2 concatenate.23
  261.9 8.0 %reshape.60 = f32[32,128,257]{2,1,0:T(8,128)} reshape(f32[32,32896]{1,0:T(8,128)} %concatenate.23) | data formatting | bytes 8421376 | tf_op jit(solution)/shard_map/reshape | solution.py:37
  269.9 1.7 slice_reduce_fusion
  271.7 72.4 %all-reduce.4 = (f32[32,128]{1,0:T(8,128)S(1)}, f32[512]{0:T(512)S(1)}) all-reduce(f32[32,128]{1,0:T(8,128)S(1)} %rev.7, f32[512]{0:T(512)S(1)} %get-tuple-element.23), channel_id=1, replica_groups=mesh['seq'=16,'tp'=16] {'seq'}, use_global_device_ids=true, to_apply=%region_3.0 | all-reduce | flops 4608 | bytes 36864 | tf_op jit(solution)/shard_map/psum | solution.py:79
  345.3 7.9 %multiply_bitcast_fusion = f32[3,512,512]{1,2,0:T(8,128)} fusion(bf16[2048,3,512]{2,0,1:T(8,128)(2,1)} %all-gather.2.cloned.1.call-done, bf16[2048,512]{1,0:T(8,128)(2,1)S(1)} %copy-done), kind=kOutput, calls=%fused_computation.1 | convolution fusion | flops 3222011904 | bytes 11534336 | tf_op jit(solution)/shard_map/tf,tjc->jfc/dot_general | solution.py:93
  353.2 3.5 copy.24
  (39 shorter events, 12.7 us)
Async XLA Ops:
  7.2 1.6 copy-start
  7.2 111.5 %reduce-scatter.3.cloned.1.call-start = ((), (), s32[]{:S(2)}) async-start(), calls=%async_computation.2 | async-start | bytes 13369344 | tf_op jit(solution)/shard_map/reduce_scatter | solution.py:51
  16.5 103.4 %copy-start.1 = (bf16[128,512]{1,0:T(8,128)(2,1)S(1)}, bf16[128,512]{1,0:T(8,128)(2,1)}, u32[]{:S(2)}) copy-start(bf16[128,512]{1,0:T(8,128)(2,1)} %param.9) | copy-start | bytes 393220
  16.5 104.8 %copy-start.2 = (f32[32,128]{1,0:T(8,128)S(1)}, f32[32,128]{1,0:T(8,128)}, u32[]{:S(2)}) copy-start(f32[32,128]{1,0:T(8,128)} %param.7) | copy-start | bytes 49156
  16.5 228.7 %all-gather.2.cloned.1.call-start = ((), (), s32[]{:S(2)}) async-start(), calls=%async_computation.3 | async-start | bytes 6684672 | tf_op jit(solution)/shard_map/all_gather | solution.py:83
  120.0 36.0 %collective-permute-start.1 = (bf16[127,512]{1,0:T(8,128)(2,1)S(1)}, bf16[127,512]{1,0:T(8,128)(2,1)S(1)}, u32[]{:S(2)}, u32[]{:S(2)}) collective-permute-start(bf16[127,512]{1,0:T(8,128)(2,1)S(1)} %slice.78), channel_id=1, source_target_pairs={{16,0},{32,16},{48,32},{64,48},{80,64},{96,80},{112,96},{128,112},... | collective-permute-start | bytes 390152 | tf_op jit(solution)/shard_map/ppermute | solution.py:10
  150.9 15.5 %collective-permute-start = (bf16[127,512]{1,0:T(8,128)(2,1)}, bf16[127,512]{1,0:T(8,128)(2,1)}, u32[]{:S(2)}, u32[]{:S(2)}) collective-permute-start(bf16[127,512]{1,0:T(8,128)(2,1)} %slice.79), channel_id=1, source_target_pairs={{0,16},{16,32},{32,48},{48,64},{64,80},{80,96},{96,112},{112,128},... | collective-permute-start | bytes 390152 | tf_op jit(solution)/shard_map/ppermute | solution.py:10
  164.6 10.9 %copy-start.3 = (f32[512]{0:T(512)S(1)}, f32[512]{0:T(512)}, u32[]{:S(2)}) copy-start(f32[512]{0:T(512)} %param.8) | copy-start | bytes 6148
  178.2 178.5 %reduce-scatter.5.cloned.1.call-start = ((), (), s32[]{:S(2)}) async-start(), calls=%async_computation.4 | async-start | bytes 2228224 | tf_op jit(solution)/shard_map/reduce_scatter | solution.py:84
Sparse Core Ops, SparseCore 0:
  16.6 102.0 reduce-scatter.2
  178.3 66.8 all-gather.1
  253.4 56.1 reduce-scatter.4
where the time goes:
time: 364 us; the launch traced here: 363 us
  waiting for transfers between devices  169 us (46%)
  blocking collectives  72.4 us (20%)
  local copies, waits for them, and re-layouts  53 us (15%)
  matrix products  38.8 us (11%)
  between operations  13.9 us (4%)
  other arithmetic  9.48 us (3%)
  starting transfers between devices  6.61 us (2%)
    reduce_scatter x1, waiting for transfers between devices, per_device(): lax.psum_scatter(project_rows(block_in, w_in), 'seq', scatter_dimension=0...  102 us
    psum x1, blocking collectives, per_device(): filt_sum, skip_sum = lax.psum((filt_part, skip_part), 'seq')  72.4 us
    all_gather x1, waiting for transfers between devices, per_device(): gathered = lax.all_gather(grads_local, 'seq', axis=0, tiled=True)  66.9 us
    reshape x2, local copies, waits for them, and re-layouts, toeplitz(): return tiled.reshape(groups_dev, slab, width - 1)  18.8 us
    unnamed x12, local copies, waits for them, and re-layouts  12.4 us
    dot_general x1, matrix products, per_device(): jnp.einsum('tjc,jfc->tf', gathered, w_in, preferred_element_type=jnp.floa...  8.01 us
    reshape x1, local copies, waits for them, and re-layouts, diagonal_sums(): skewed = flat.reshape(groups_dev, slab, width + 1)[:, :, :taps]  7.96 us
    dot_general x1, matrix products, per_device(): jnp.einsum('tf,tjc->jfc', block_in, gathered, preferred_element_type=jnp....  7.95 us
  transfers between devices with their start and end apart: 5, of which 2 were waited for; matrix products, arithmetic and copies ran while one was open for 20% of the time, Pallas kernels for 0%

commit v1 on v0

v1 whole, which is shorter than its diff:
```python
import functools

import jax
import jax.numpy as jnp
from jax import lax
from jax.experimental import pallas as pl
from jax.experimental.pallas import tpu as pltpu
from jax.sharding import PartitionSpec as P

MESH = pl.DeviceIdType.MESH
F32 = jnp.float32
BF16 = jnp.bfloat16
HIGHEST = lax.Precision.HIGHEST
N_SEMS = 256
QUARTER = 512


def dot_nt(a, b, precision=None):
    return lax.dot_general(a, b, (((1,), (1,)), ((), ())), precision=precision, preferred_element_type=F32)


def dot_nn(a, b, precision=None):
    return lax.dot_general(a, b, (((1,), (0,)), ((), ())), precision=precision, preferred_element_type=F32)


def block_kernel(
    scale, bi, w, filt, skip, gy, bo_out, gx_out, gw_out, gf_out, gs_out,
    wt, bit, part, r1, r2, gath, gx, gyt, gy1, gy2, bo0, bo1, bo2, sm, cs, cr, zs, zr, ssem, rsem,
):
    seq, tp = lax.axis_index("seq"), lax.axis_index("tp")
    x, y, z, core = lax.rem(seq, 4), lax.div(seq, 4), lax.div(tp, 2), lax.rem(tp, 2)

    def m4(v):
        return lax.rem(v + 4, 4)

    def m8(v):
        return lax.rem(v + 8, 8)

    def at_x(by):
        return (y * 4 + m4(x + by), tp)

    def at_y(by):
        return (m4(y + by) * 4 + x, tp)

    def at_z(by):
        return (seq, m8(z + by) * 2 + core)

    at_core = (seq, z * 2 + (1 - core))
    partners = [at_x(1), at_x(-1), at_x(2), at_y(1), at_y(-1), at_y(2), at_z(1), at_z(-1), at_core]

    barrier = pltpu.get_barrier_semaphore()
    for device in partners:
        pl.semaphore_signal(barrier, inc=1, device_id=device, device_id_type=MESH)

    sent = []

    def send(src, dst, device):
        k = len(sent)
        copy = pltpu.make_async_remote_copy(
            src_ref=src, dst_ref=dst, send_sem=ssem.at[k], recv_sem=rsem.at[k], device_id=device, device_id_type=MESH
        )
        copy.start()
        sent.append(copy)
        return copy

    def transpose_w(g):
        for j in range(3):
            wt[j, g * 256 : (g + 1) * 256, :] = w[j, :, g * 256 : (g + 1) * 256].T

    def transpose_bi():
        @pl.loop(0, 4)
        def _(i):
            rows = pl.ds(pl.multiple_of(i * 512, 512), 512)
            bit[:, rows] = bi[rows, :].T

    def project(g):
        @pl.loop(0, 4)
        def _(i):
            rows = pl.ds(pl.multiple_of(i * 512, 512), 512)
            tokens = bi[rows, :]
            for j in range(3):
                p = dot_nt(wt[j, g * 256 : (g + 1) * 256, :], tokens).astype(BF16)
                part[g, j, :, :, :, rows] = p.reshape(4, 4, 16, 512)

    def grad_x_quarter(g, i):
        rows = pl.ds(i * QUARTER, QUARTER)
        total = None
        for j in range(3):
            d = gath[g, j, :, :, :, rows].reshape(256, QUARTER)
            p = dot_nn(w[j, :, g * 256 : (g + 1) * 256], d)
            total = p if total is None else total + p
        if g == 0:
            gx[:, rows] = total
        else:
            gx[:, rows] += total

    def grad_w(g, j):
        for i in range(2):
            d = gath[g, j].reshape(256, 2048)
            gw_out[j, i * 256 : (i + 1) * 256, g * 256 : (g + 1) * 256] = dot_nt(bit[i * 256 : (i + 1) * 256, :], d) * scale

    pos_big, pos_small = (x, y), (y, x)
    big_dev, small_dev = (at_x, at_y), (at_y, at_x)

    def big(ref, g, h, q, start, size):
        tokens = pl.ds(h * 1024 + start, size)
        return ref.at[g, :, :, q, :, tokens] if h == 0 else ref.at[g, :, q, :, :, tokens]

    def one(ref, g, h, q_big, q_small, start, size):
        tokens = pl.ds(h * 1024 + start, size)
        return ref.at[g, :, q_small, q_big, :, tokens] if h == 0 else ref.at[g, :, q_big, q_small, :, tokens]

    def small(g, h, q, start, size):
        return one(part, g, h, pos_big[h], q, start, size)

    BY = (1, -1)
    FAR = (0, QUARTER)
    NEAR = (QUARTER, 0)

    def add_big(dst, *srcs):
        @pl.loop(0, 3)
        def _(j):
            for i in range(4):
                total = dst[j, i].astype(F32)
                for s in srcs:
                    total = total + s[j, i].astype(F32)
                dst[j, i] = total.astype(BF16)

    def add_small(dst, *srcs):
        for j in range(3):
            total = dst[j].astype(F32)
            for s in srcs:
                total = total + s[j].astype(F32)
            dst[j] = total.astype(BF16)

    s1, s2a, s2b, t1, t2a, t2b = {}, {}, {}, {}, {}, {}

    def send_s1(g):
        for h in range(2):
            for d in range(2):
                src = big(part, g, h, m4(pos_big[h] + 2), FAR[d], QUARTER)
                s1[g, h, d] = send(src, r1.at[g, h, d, 0], big_dev[h](BY[d]))

    def send_s2a(g):
        for h in range(2):
            for d in range(2):
                src = big(part, g, h, m4(pos_big[h] + BY[d]), NEAR[d], QUARTER)
                s2a[g, h, d] = send(src, r1.at[g, h, d, 1], big_dev[h](BY[d]))

    def send_s2b(g):
        for h in range(2):
            for d in range(2):
                src = big(part, g, h, m4(pos_big[h] + BY[d]), FAR[d], QUARTER)
                s1[g, h, d].wait_recv()
                add_big(src, r1.at[g, h, d, 0])
                s2b[g, h, d] = send(src, r1.at[g, h, d, 2], big_dev[h](BY[d]))

    def finish_big(g):
        for h in range(2):
            for d in range(2):
                s2a[g, h, d].wait_recv()
        for h in range(2):
            for d in range(2):
                s2b[g, h, d].wait_recv()
                add_big(big(part, g, h, pos_big[h], FAR[d], QUARTER), r1.at[g, h, d, 2], r1.at[g, h, 1 - d, 1])
                t1[g, h, d] = send(small(g, h, m4(pos_small[h] + 2), FAR[d], QUARTER), r2.at[g, h, d, 0], small_dev[h](BY[d]))
                src = small(g, h, m4(pos_small[h] + BY[1 - d]), FAR[d], QUARTER)
                t2a[g, h, 1 - d] = send(src, r2.at[g, h, 1 - d, 1], small_dev[h](BY[1 - d]))

    def send_t2b(g):
        for h in range(2):
            for d in range(2):
                t1[g, h, d].wait_recv()
                src = small(g, h, m4(pos_small[h] + BY[d]), FAR[d], QUARTER)
                add_small(src, r2.at[g, h, d, 0])
                t2b[g, h, d] = send(src, r2.at[g, h, d, 2], small_dev[h](BY[d]))

    def filter_group(g):
        for h in range(2):
            for d in range(2):
                t2a[g, h, d].wait_recv()
                t2b[g, h, d].wait_recv()

        def stacked(j):
            pieces = []
            for b in range(16):
                h, d, o = b // 8, (b % 8) // 4, (b % 4) * 128
                total = part[g, j, y, x, :, b * 128 : (b + 1) * 128].astype(F32)
                total = total + r2[g, h, d, 2, j, :, o : o + 128].astype(F32)
                total = total + r2[g, h, 1 - d, 1, j, :, o : o + 128].astype(F32)
                pieces.append(total.astype(BF16).astype(F32))
            return jnp.concatenate(pieces, axis=0)

        gate, key, value = stacked(0), stacked(1), stacked(2)
        u = key * value
        blank = jnp.zeros((16, 128), F32)
        u_ext = jnp.concatenate([jnp.concatenate([blank, u[:240]], axis=0), u], axis=1)
        taps = jnp.broadcast_to(filt[pl.ds(g * 16 + seq, 1), :], (256, 128))
        taps = jnp.concatenate([taps, jnp.zeros((256, 128), F32)], axis=1)
        causal = pltpu.roll(taps, 128, 1, stride=1, stride_axis=0)[:, :128]
        anti = pltpu.roll(taps[:128], 0, 1, stride=1, stride_axis=0)

        lane = lax.broadcasted_iota(jnp.int32, (16, 512), 1)
        row = lax.broadcasted_iota(jnp.int32, (16, 512), 0)
        mine = lane == row + (g * 256 + seq * 16)
        skip_col = jnp.sum(jnp.where(mine, jnp.broadcast_to(skip[...], (16, 512)), 0.0), axis=1, keepdims=True)
        skip_all = jnp.concatenate([jnp.broadcast_to(skip_col, (16, 128))] * 16, axis=0)

        z_val = dot_nn(u_ext, causal, HIGHEST) + skip_all * u
        g_y = jnp.concatenate([gy2[b // 4, b % 4, g] for b in range(16)], axis=0).astype(F32)
        dz = g_y * gate
        dz_ext = jnp.concatenate([dz, jnp.concatenate([dz[16:], blank], axis=0)], axis=1)
        du = dot_nt(dz_ext, anti, HIGHEST) + skip_all * dz

        def keep(j, value_of):
            v = value_of.astype(BF16)
            for b in range(16):
                gath[g, j, y, x, :, b * 128 : (b + 1) * 128] = v[b * 16 : (b + 1) * 16]

        keep(0, g_y * z_val)
        keep(1, du * value)
        keep(2, du * key)
        out = (gate * z_val).astype(BF16)
        for b in range(16):
            bo0[g, b // 4, b % 4] = out[b * 16 : (b + 1) * 16]

        def sums():
            flip = (lax.broadcasted_iota(jnp.int32, (128, 128), 0) + lax.broadcasted_iota(jnp.int32, (128, 128), 1)) == 127
            dz_back = dot_nt(jnp.where(flip, 1.0, 0.0).astype(F32), dz, HIGHEST)
            lagged = pltpu.roll(dot_nn(dz_back, u_ext, HIGHEST), 129, 1, stride=1, stride_axis=0)
            by_lag = jnp.broadcast_to(jnp.sum(lagged, axis=0, keepdims=True), (8, 256))
            lag_rows = lax.broadcasted_iota(jnp.int32, (256, 128), 0)
            lag_cols = lax.broadcasted_iota(jnp.int32, (256, 128), 1)
            pick = jnp.where(lag_rows + lag_cols == 128, 1.0, 0.0).astype(F32)
            sm[y, x, g : g + 1, :] = dot_nn(by_lag, pick, HIGHEST)[:1] * scale
            product = dz * u
            folded = product[:16]
            for b in range(1, 16):
                folded = folded + product[b * 16 : (b + 1) * 16]
            per_ch = jnp.sum(folded, axis=1, keepdims=True) * scale
            placed = jnp.sum(jnp.where(mine, jnp.broadcast_to(per_ch, (16, 512)), 0.0), axis=0, keepdims=True)
            for i in range(2):
                o = g * 256 + i * 128
                sm[y, x, 4 + g * 2 + i : 5 + g * 2 + i, :] = placed[:, o : o + 128]

        return sums

    u1, u2, v1, v2 = {}, {}, {}, {}

    def ag_send(table, key, g, h, q_big, q_small, start, size, device):
        ref = one(gath, g, h, q_big, q_small, start, size)
        table[key] = send(ref, ref, device)

    def ag_open(g):
        for h in range(2):
            for d in range(2):
                ag_send(u1, (g, h, d), g, h, pos_big[h], pos_small[h], 0, 1024, small_dev[h](BY[d]))
        for h in range(2):
            for d in range(2):
                ag_send(v1, (g, h, 0, d), g, h, pos_big[h], pos_small[h], 0, 1024, big_dev[h](BY[d]))

    def ag_near(g):
        for h in range(2):
            for d in range(2):
                u1[g, h, d].wait_recv()
                ag_send(u2, (g, h, d), g, h, pos_big[h], m4(pos_small[h] - BY[d]), FAR[d], QUARTER, small_dev[h](BY[d]))
        for h in range(2):
            for e in range(2):
                for d in range(2):
                    ag_send(v1, (g, h, 1 + e, d), g, h, pos_big[h], m4(pos_small[h] - BY[e]), 0, 1024, big_dev[h](BY[d]))

    def ag_far(g):
        for h in range(2):
            for d in range(2):
                u2[g, h, d].wait_recv()
            for d in range(2):
                ag_send(v1, (g, h, 3, d), g, h, pos_big[h], m4(pos_small[h] + 2), 0, 1024, big_dev[h](BY[d]))

    def ag_forward(g, piece):
        for h in range(2):
            q = m4(pos_small[h] + (0, -1, 1, 2)[piece])
            for d in range(2):
                v1[g, h, piece, d].wait_recv()
                ag_send(v2, (g, h, piece, d), g, h, m4(pos_big[h] - BY[d]), q, FAR[d], QUARTER, big_dev[h](BY[d]))

    def ag_close(g):
        for h in range(2):
            for piece in range(4):
                for d in range(2):
                    v2[g, h, piece, d].wait_recv()

    def bo_first(g):
        own = bo0[g, y]
        bo1[g, y] = own
        return [send(bo0.at[g, m4(y + k)], bo1.at[g, y], at_y(k)) for k in (1, -1, 2)]

    def bo_second(g, arriving):
        for copy in arriving:
            copy.wait_recv()
        bo2[g, x] = bo1[g, :, x]
        return [send(bo1.at[g, :, m4(x + k)], bo2.at[g, x], at_x(k)) for k in (1, -1, 2)]

    def bo_last(g, arriving):
        for copy in arriving:
            copy.wait_recv()
        rows = jnp.concatenate([bo2[g, d % 4, d // 4] for d in range(16)], axis=0)
        bo_out[:, g * 256 : (g + 1) * 256] = rows.T

    gy_t = gy[...].T
    for g in range(2):
        for d in range(16):
            gyt[d % 4, d // 4, g] = gy_t[g * 256 + d * 16 : g * 256 + (d + 1) * 16]
    gy1[x] = gyt[x]
    transpose_w(0)
    project(0)
    pl.semaphore_wait(barrier, len(partners))
    gy_a = [send(gyt.at[m4(x + k)], gy1.at[x], at_x(k)) for k in (1, -1, 2)]
    send_s1(0)
    send_s2a(0)
    transpose_w(1)
    project(1)
    for copy in gy_a:
        copy.wait_recv()
    gy2[y] = gy1[:, y]
    gy_b = [send(gy1.at[:, m4(y + k)], gy2.at[y], at_y(k)) for k in (1, -1, 2)]
    send_s2b(0)
    transpose_bi()
    send_s1(1)
    sm[y, x] = jnp.zeros((8, 128), F32)
    finish_big(0)
    send_s2a(1)
    send_t2b(0)
    send_s2b(1)
    for copy in gy_b:
        copy.wait_recv()
    sums0 = filter_group(0)
    ag_open(0)
    sums0()
    finish_big(1)
    ag_near(0)
    bo_a0 = bo_first(0)
    send_t2b(1)
    ag_forward(0, 0)
    ag_far(0)
    bo_b0 = bo_second(0, bo_a0)
    sums1 = filter_group(1)
    ag_open(1)
    sums1()
    ag_forward(0, 1)
    ag_forward(0, 2)
    ag_near(1)
    ag_forward(0, 3)
    ag_far(1)
    bo_a1 = bo_first(1)
    sm_a = [send(sm.at[y, x], sm.at[y, x], at_y(k)) for k in (1, -1, 2)]
    ag_close(0)
    ag_forward(1, 0)
    grad_x_quarter(0, 0)
    grad_x_quarter(0, 1)
    ag_forward(1, 1)
    ag_forward(1, 2)
    grad_x_quarter(0, 2)
    grad_x_quarter(0, 3)
    bo_b1 = bo_second(1, bo_a1)
    for copy in sm_a:
        copy.wait_recv()
    sm_b = [send(sm.at[:, x], sm.at[:, x], at_x(k)) for k in (1, -1, 2)]
    ag_forward(1, 3)
    for j in range(3):
        grad_w(0, j)
    ag_close(1)

    order = (4, 3, -3, 2, -2, 1, -1, 0)
    pair = {}
    gx_other = [None] * 8
    for i in range(4):
        grad_x_quarter(1, i)
    for k in order:
        q = m8(z + k)
        theirs = pl.ds(pl.multiple_of((q * 2 + (1 - core)) * 128, 128), 128)
        cs[q] = gx[:, theirs].astype(BF16)
        pair[k] = send(cs.at[q], cr.at[q], at_core)

    def pair_sum(k):
        q = m8(z + k)
        own = pl.ds(pl.multiple_of((q * 2 + core) * 128, 128), 128)
        pair[k].wait_recv()
        zs[q] = (gx[:, own] + cr[q].astype(F32)).astype(BF16)

    ring = {}
    FARZ, NEARZ = (0, 256), (256, 0)

    def z_send(d, k, far, received):
        q = m8(z + BY[d] * k)
        r = (FARZ if far else NEARZ)[d]
        slot = (4 - k) if far else (4 + 3 - k)
        if received:
            prev = ring[d, k + 1, far]
            prev.wait_recv()
            rows = zs.at[q, r : r + 256]
            zs[q, r : r + 256] = (rows[...].astype(F32) + zr[d, slot - 1].astype(F32)).astype(BF16)
        ring[d, k, far] = send(zs.at[q, pl.ds(r, 256)], zr.at[d, slot], at_z(BY[d]))

    pair_sum(4)
    for d in range(2):
        z_send(d, 4, True, False)
    pair_sum(3)
    pair_sum(-3)
    for d in range(2):
        z_send(d, 3, False, False)
    for k in order[3:]:
        pair_sum(k)
    for d in range(2):
        z_send(d, 3, True, True)
    grad_w(1, 0)
    for k in (2, 1):
        for far in (False, True):
            for d in range(2):
                z_send(d, k, far, True)
        grad_w(1, 3 - k)
    bo_last(0, bo_b0)
    bo_last(1, bo_b1)
    for copy in sm_b:
        copy.wait_recv()
    for g in range(2):
        for d in range(16):
            gf_out[g * 16 + d : g * 16 + d + 1, :] = sm[d // 4, d % 4, g : g + 1, :]
    skips = sm[0, 0, 4:8, :]
    for d in range(1, 16):
        skips = skips + sm[d // 4, d % 4, 4:8, :]
    gs_out[...] = skips

    for far, rows in ((False, 0), (True, 0)):
        for d in range(2):
            ring[d, 1, far].wait_recv()
    own = zs[z]
    top = own[:256].astype(F32) + zr[0, 3].astype(F32) + zr[1, 6].astype(F32)
    low = own[256:].astype(F32) + zr[1, 3].astype(F32) + zr[0, 6].astype(F32)
    gx_out[:, :256] = top.T.astype(BF16)
    gx_out[:, 256:] = low.T.astype(BF16)
    for copy in sent:
        copy.wait_send()


def per_device(block_in, w_in, filt, skip, grad_y):
    tokens = block_in.shape[0]
    scale = tokens ** (-0.5)
    vmem = pl.BlockSpec(memory_space=pltpu.VMEM)
    out_shape = (
        jax.ShapeDtypeStruct((128, 512), BF16),
        jax.ShapeDtypeStruct((128, 512), BF16),
        jax.ShapeDtypeStruct((3, 512, 512), F32),
        jax.ShapeDtypeStruct((32, 128), F32),
        jax.ShapeDtypeStruct((4, 128), F32),
    )
    scratch = [
        pltpu.VMEM((3, 512, 512), BF16),
        pltpu.VMEM((512, 2048), BF16),
        pltpu.VMEM((2, 3, 4, 4, 16, 2048), BF16),
        pltpu.VMEM((2, 2, 2, 3, 3, 4, 16, QUARTER), BF16),
        pltpu.VMEM((2, 2, 2, 3, 3, 16, QUARTER), BF16),
        pltpu.VMEM((2, 3, 4, 4, 16, 2048), BF16),
        pltpu.VMEM((512, 2048), F32),
        pltpu.VMEM((4, 4, 2, 16, 128), BF16),
        pltpu.VMEM((4, 4, 2, 16, 128), BF16),
        pltpu.VMEM((4, 4, 2, 16, 128), BF16),
        pltpu.VMEM((2, 4, 4, 16, 128), BF16),
        pltpu.VMEM((2, 4, 4, 16, 128), BF16),
        pltpu.VMEM((2, 4, 4, 16, 128), BF16),
        pltpu.VMEM((4, 4, 8, 128), F32),
        pltpu.VMEM((8, 512, 128), BF16),
        pltpu.VMEM((8, 512, 128), BF16),
        pltpu.VMEM((8, 512, 128), BF16),
        pltpu.VMEM((2, 7, 256, 128), BF16),
        pltpu.SemaphoreType.DMA((N_SEMS,)),
        pltpu.SemaphoreType.DMA((N_SEMS,)),
    ]
    block_out, grad_x, grad_w, grad_filt, grad_skip = pl.pallas_call(
        functools.partial(block_kernel, scale),
        out_shape=out_shape,
        in_specs=[vmem] * 5,
        out_specs=[vmem] * 5,
        scratch_shapes=scratch,
        compiler_params=pltpu.CompilerParams(
            collective_id=0, has_side_effects=True, vmem_limit_bytes=60 * 2**20
        ),
        cost_estimate=pl.CostEstimate(flops=10**10, bytes_accessed=10**7, transcendentals=0),
    )(block_in, w_in, filt, skip.reshape(1, 512), grad_y)
    return block_out, grad_x, grad_w, grad_filt, grad_skip.reshape(512)


def solution(mesh):
    in_specs = (P(None, "seq"), P(None, "seq", "tp"), P("tp", None), P("tp"), P("seq", "tp"))
    out_specs = (P("seq", "tp"), P("tp", "seq"), P(None, "seq", "tp"), P("tp", None), P("tp"))
    return jax.shard_map(per_device, mesh=mesh, in_specs=in_specs, out_specs=out_specs, check_vma=False)
```

time: 364 us -> 116 us (0.32)
  waiting for transfers between devices: 169 us -> 0 us
  Pallas kernels: 0 us -> 105 us
  blocking collectives: 72.4 us -> 0 us
  local copies, waits for them, and re-layouts: 53 us -> 8.2 us
  matrix products: 38.8 us -> 0 us
  between operations: 13.9 us -> 0.65 us
  other arithmetic: 9.48 us -> 0 us
  starting transfers between devices: 6.61 us -> 0 us
    pallas_call x0 -> x1, Pallas kernels: none -> 105 us  [per_device(): pl.pallas_call(functools.partial(block_kernel, scale), out_shape=out_shap...]
    reduce_scatter x2 -> x0, waiting for transfers between devices: 102 us -> none  [the longest x1 102 us: per_device(): lax.psum_scatter(project_rows(block_in, w_in), 'seq', scatter_dimension=0...]
    psum x1 -> x0, blocking collectives: 72.4 us -> none  [per_device(): filt_sum, skip_sum = lax.psum((filt_part, skip_part), 'seq')]
    all_gather x1 -> x0, waiting for transfers between devices: 66.9 us -> none  [per_device(): gathered = lax.all_gather(grads_local, 'seq', axis=0, tiled=True)]
    dot_general x6 -> x0, matrix products: 38.8 us -> none  [the longest x1 8.01 us: per_device(): jnp.einsum('tjc,jfc->tf', gathered, w_in, preferred_element_type=jnp.floa...]
    reshape x5 -> x0, local copies, waits for them, and re-layouts: 29.4 us -> none  [the longest x2 18.8 us: toeplitz(): return tiled.reshape(groups_dev, slab, width - 1)]
    ppermute x2 -> x0, starting transfers between devices: 6.49 us -> none  [passed_along(): return lax.ppermute(array, axis, pairs)]
    concatenate x6 -> x0, local copies, waits for them, and re-layouts: 5.12 us -> none  [the longest x1 2.21 us: diagonal_sums(): jnp.concatenate([padded.reshape(groups_dev, slab * width), jnp.zeros((gro...]
  transfers between devices with their start and end apart: 5 -> 0, of which waited for: 2 -> 0; matrix products, arithmetic and copies ran while one was open for 20% -> 0% of each run, Pallas kernels for 0% -> 0%
where the time goes in v1:
time: 116 us; the launch traced here: 114 us
  Pallas kernels  105 us (91%)
  local copies, waits for them, and re-layouts  8.2 us (7%)
    pallas_call x1, Pallas kernels, per_device(): pl.pallas_call(functools.partial(block_kernel, scale), out_shape=out_shap...  105 us
    unnamed x9, local copies, waits for them, and re-layouts  8.2 us

profile of v1, /device:TPU:32, one launch (start us, length us, event | category | flops | bytes accessed | tf_op | source)
XLA Modules:
  0.0 114.0 jit_solution(51623872380615880)
XLA Ops:
  0.6 105.2 %shard_map.92 = (bf16[128,512]{1,0:T(8,128)(2,1)}, bf16[128,512]{1,0:T(8,128)(2,1)}, f32[3,512,512]{2,1,0:T(8,128)}, f32[32,128]{1,0:T(8,128)}, f32[4,128]{1,0:T(4,128)}) custom-call(bf16[2048,512]{1,0:T(8,128)(2,1)} %bi.1, bf16[3,512,512]{2,1,0:T(8,128)(2,1)} %w.1, f32[32,128]{1,0:T(8,128)} %filt.1, f32[1,512]{1,0:T(1,128)} %bitcast.3, bf16[128,512]{1,0:T(8,128)(2,1)} %gy.1), custom_call_target="tpu_custom_call" | custom-call | flops 10000000000 | bytes 10000000 | tf_op jit(solution)/shard_map/pallas_call | solution.py:478
  105.8 1.6 %copy.15 = bf16[128,512]{1,0:T(8,128)(2,1)} copy(bf16[128,512]{1,0:T(8,128)(2,1)} %get-tuple-element.20) | data formatting | bytes 262144
  107.4 1.6 %copy.16 = bf16[128,512]{1,0:T(8,128)(2,1)} copy(bf16[128,512]{1,0:T(8,128)(2,1)} %get-tuple-element.21) | data formatting | bytes 262144
  109.0 0.0 copy-start
  109.0 0.0 copy-start.1
  109.0 3.9 %copy.17 = f32[3,512,512]{2,1,0:T(8,128)} copy(f32[3,512,512]{2,1,0:T(8,128)} %get-tuple-element.22) | data formatting | bytes 6291456
  112.8 0.0 copy-done
  112.8 0.6 copy.18
  113.4 0.0 copy-done.1
  113.4 0.6 copy.19
Async XLA Ops:
  109.0 3.9 %copy-start = (f32[32,128]{1,0:T(8,128)S(1)}, f32[32,128]{1,0:T(8,128)}, u32[]{:S(2)}) copy-start(f32[32,128]{1,0:T(8,128)} %get-tuple-element.23) | copy-start | bytes 49156
  109.0 4.5 %copy-start.1 = (f32[4,128]{1,0:T(4,128)S(1)}, f32[4,128]{1,0:T(4,128)}, u32[]{:S(2)}) copy-start(f32[4,128]{1,0:T(4,128)} %get-tuple-element.14) | copy-start | bytes 6148

commit v2 on v1

--- a/solution.py
+++ b/solution.py
@@ -24,8 +24,8 @@
 
 
 def block_kernel(
-    scale, bi, w, filt, skip, gy, bo_out, gx_out, gw_out, gf_out, gs_out,
-    wt, bit, part, r1, r2, gath, gx, gyt, gy1, gy2, bo0, bo1, bo2, sm, cs, cr, zs, zr, ssem, rsem,
+    scale, bi_in, w_in, filt, skip, gy, bo_out, gx_out, gw_out, gf_out, gs_out,
+    bi, w, wt, bit, part, r1, r2, gath, gx, gyt, gy1, gy2, bo0, bo1, bo2, sm, cs, cr, zs, zr, ssem, rsem, lsem,
 ):
     seq, tp = lax.axis_index("seq"), lax.axis_index("tp")
     x, y, z, core = lax.rem(seq, 4), lax.div(seq, 4), lax.div(tp, 2), lax.rem(tp, 2)
@@ -51,6 +51,17 @@
     barrier = pltpu.get_barrier_semaphore()
     for device in partners:
         pl.semaphore_signal(barrier, inc=1, device_id=device, device_id_type=MESH)
+
+    def load(src, dst, k):
+        copy = pltpu.make_async_copy(src, dst, lsem.at[k])
+        copy.start()
+        return copy
+
+    half_w = [pl.ds(0, 256), pl.ds(256, 256)]
+    quarter = [pl.ds(i * QUARTER, QUARTER) for i in range(4)]
+    w_load = [load(w_in.at[:, :, half_w[0]], w.at[:, :, half_w[0]], 0)]
+    bi_load = [load(bi_in.at[q], bi.at[q], 2 + i) for i, q in enumerate(quarter)]
+    w_load.append(load(w_in.at[:, :, half_w[1]], w.at[:, :, half_w[1]], 1))
 
     sent = []
 
@@ -73,31 +84,35 @@
             rows = pl.ds(pl.multiple_of(i * 512, 512), 512)
             bit[:, rows] = bi[rows, :].T
 
+    def project_rows(g, rows):
+        tokens = bi[rows, :]
+        for j in range(3):
+            p = dot_nt(wt[j, g * 256 : (g + 1) * 256, :], tokens).astype(BF16)
+            part[g, j, :, :, :, rows] = p.reshape(4, 4, 16, 512)
+
     def project(g):
         @pl.loop(0, 4)
         def _(i):
-            rows = pl.ds(pl.multiple_of(i * 512, 512), 512)
-            tokens = bi[rows, :]
-            for j in range(3):
-                p = dot_nt(wt[j, g * 256 : (g + 1) * 256, :], tokens).astype(BF16)
-                part[g, j, :, :, :, rows] = p.reshape(4, 4, 16, 512)
-
-    def grad_x_quarter(g, i):
-        rows = pl.ds(i * QUARTER, QUARTER)
+            project_rows(g, pl.ds(pl.multiple_of(i * 512, 512), 512))
+
+    def grad_x_near(i):
+        rows = quarter[i]
         total = None
         for j in range(3):
-            d = gath[g, j, :, :, :, rows].reshape(256, QUARTER)
-            p = dot_nn(w[j, :, g * 256 : (g + 1) * 256], d)
+            p = dot_nn(w[j, :, :256], gath[0, j, :, :, :, rows].reshape(256, QUARTER))
             total = p if total is None else total + p
-        if g == 0:
-            gx[:, rows] = total
-        else:
-            gx[:, rows] += total
-
-    def grad_w(g, j):
-        for i in range(2):
-            d = gath[g, j].reshape(256, 2048)
-            gw_out[j, i * 256 : (i + 1) * 256, g * 256 : (g + 1) * 256] = dot_nt(bit[i * 256 : (i + 1) * 256, :], d) * scale
+        gx[:, rows] = total
+
+    def grad_x_chunk(q):
+        rows = pl.ds(pl.multiple_of(q * 256, 256), 256)
+        total = gx[:, rows]
+        for j in range(3):
+            total = total + dot_nn(w[j, :, 256:], gath[1, j, :, :, :, rows].reshape(256, 256))
+        gx[:, rows] = total
+
+    def grad_w(g, j, i):
+        d = gath[g, j].reshape(256, 2048)
+        gw_out[j, i * 256 : (i + 1) * 256, half_w[g]] = dot_nt(bit[i * 256 : (i + 1) * 256, :], d) * scale
 
     pos_big, pos_small = (x, y), (y, x)
     big_dev, small_dev = (at_x, at_y), (at_y, at_x)
@@ -135,11 +150,14 @@
 
     s1, s2a, s2b, t1, t2a, t2b = {}, {}, {}, {}, {}, {}
 
+    def send_s1_one(g, h, d):
+        src = big(part, g, h, m4(pos_big[h] + 2), FAR[d], QUARTER)
+        s1[g, h, d] = send(src, r1.at[g, h, d, 0], big_dev[h](BY[d]))
+
     def send_s1(g):
         for h in range(2):
             for d in range(2):
-                src = big(part, g, h, m4(pos_big[h] + 2), FAR[d], QUARTER)
-                s1[g, h, d] = send(src, r1.at[g, h, d, 0], big_dev[h](BY[d]))
+                send_s1_one(g, h, d)
 
     def send_s2a(g):
         for h in range(2):
@@ -222,7 +240,7 @@
         keep(2, du * key)
         out = (gate * z_val).astype(BF16)
         for b in range(16):
-            bo0[g, b // 4, b % 4] = out[b * 16 : (b + 1) * 16]
+            bo0[b // 4, g, b % 4] = out[b * 16 : (b + 1) * 16]
 
         def sums():
             flip = (lax.broadcasted_iota(jnp.int32, (128, 128), 0) + lax.broadcasted_iota(jnp.int32, (128, 128), 1)) == 127
@@ -289,44 +307,48 @@
                 for d in range(2):
                     v2[g, h, piece, d].wait_recv()
 
-    def bo_first(g):
-        own = bo0[g, y]
-        bo1[g, y] = own
-        return [send(bo0.at[g, m4(y + k)], bo1.at[g, y], at_y(k)) for k in (1, -1, 2)]
-
-    def bo_second(g, arriving):
+    def bo_first():
+        bo1[y] = bo0[y]
+        return [send(bo0.at[m4(y + k)], bo1.at[y], at_y(k)) for k in (1, -1, 2)]
+
+    def bo_second(arriving):
         for copy in arriving:
             copy.wait_recv()
-        bo2[g, x] = bo1[g, :, x]
-        return [send(bo1.at[g, :, m4(x + k)], bo2.at[g, x], at_x(k)) for k in (1, -1, 2)]
-
-    def bo_last(g, arriving):
+        bo2[x] = bo1[:, :, x]
+        return [send(bo1.at[:, :, m4(x + k)], bo2.at[x], at_x(k)) for k in (1, -1, 2)]
+
+    def bo_last(arriving):
         for copy in arriving:
             copy.wait_recv()
-        rows = jnp.concatenate([bo2[g, d % 4, d // 4] for d in range(16)], axis=0)
-        bo_out[:, g * 256 : (g + 1) * 256] = rows.T
+        for g in range(2):
+            rows = jnp.concatenate([bo2[d % 4, d // 4, g] for d in range(16)], axis=0)
+            bo_out[:, g * 256 : (g + 1) * 256] = rows.T
 
     gy_t = gy[...].T
     for g in range(2):
         for d in range(16):
             gyt[d % 4, d // 4, g] = gy_t[g * 256 + d * 16 : g * 256 + (d + 1) * 16]
     gy1[x] = gyt[x]
+    sm[y, x] = jnp.zeros((8, 128), F32)
+    w_load[0].wait()
     transpose_w(0)
-    project(0)
     pl.semaphore_wait(barrier, len(partners))
     gy_a = [send(gyt.at[m4(x + k)], gy1.at[x], at_x(k)) for k in (1, -1, 2)]
-    send_s1(0)
+    for i in range(4):
+        bi_load[i].wait()
+        project_rows(0, quarter[i])
+        send_s1_one(0, i // 2, i % 2)
     send_s2a(0)
+    w_load[1].wait()
     transpose_w(1)
-    project(1)
     for copy in gy_a:
         copy.wait_recv()
     gy2[y] = gy1[:, y]
     gy_b = [send(gy1.at[:, m4(y + k)], gy2.at[y], at_y(k)) for k in (1, -1, 2)]
+    project(1)
     send_s2b(0)
+    send_s1(1)
     transpose_bi()
-    send_s1(1)
-    sm[y, x] = jnp.zeros((8, 128), F32)
     finish_big(0)
     send_s2a(1)
     send_t2b(0)
@@ -338,11 +360,9 @@
     sums0()
     finish_big(1)
     ag_near(0)
-    bo_a0 = bo_first(0)
     send_t2b(1)
     ag_forward(0, 0)
     ag_far(0)
-    bo_b0 = bo_second(0, bo_a0)
     sums1 = filter_group(1)
     ag_open(1)
     sums1()
@@ -351,32 +371,31 @@
     ag_near(1)
     ag_forward(0, 3)
     ag_far(1)
-    bo_a1 = bo_first(1)
-    sm_a = [send(sm.at[y, x], sm.at[y, x], at_y(k)) for k in (1, -1, 2)]
     ag_close(0)
     ag_forward(1, 0)
-    grad_x_quarter(0, 0)
-    grad_x_quarter(0, 1)
+    sm_a = [send(sm.at[y, x], sm.at[y, x], at_y(k)) for k in (1, -1, 2)]
+    grad_x_near(0)
+    grad_x_near(1)
     ag_forward(1, 1)
     ag_forward(1, 2)
-    grad_x_quarter(0, 2)
-    grad_x_quarter(0, 3)
-    bo_b1 = bo_second(1, bo_a1)
+    grad_x_near(2)
+    grad_x_near(3)
     for copy in sm_a:
         copy.wait_recv()
     sm_b = [send(sm.at[:, x], sm.at[:, x], at_x(k)) for k in (1, -1, 2)]
     ag_forward(1, 3)
     for j in range(3):
-        grad_w(0, j)
+        for i in range(2):
+            grad_w(0, j, i)
     ag_close(1)
 
     order = (4, 3, -3, 2, -2, 1, -1, 0)
-    pair = {}
-    gx_other = [None] * 8
-    for i in range(4):
-        grad_x_quarter(1, i)
-    for k in order:
+    pair, ring = {}, {}
+    FARZ, NEARZ = (0, 256), (256, 0)
+
+    def pair_send(k):
         q = m8(z + k)
+        grad_x_chunk(q)
         theirs = pl.ds(pl.multiple_of((q * 2 + (1 - core)) * 128, 128), 128)
         cs[q] = gx[:, theirs].astype(BF16)
         pair[k] = send(cs.at[q], cr.at[q], at_core)
@@ -387,39 +406,54 @@
         pair[k].wait_recv()
         zs[q] = (gx[:, own] + cr[q].astype(F32)).astype(BF16)
 
-    ring = {}
-    FARZ, NEARZ = (0, 256), (256, 0)
-
-    def z_send(d, k, far, received):
+    def z_send(d, k, far):
         q = m8(z + BY[d] * k)
-        r = (FARZ if far else NEARZ)[d]
+        first = k == (4 if far else 3)
         slot = (4 - k) if far else (4 + 3 - k)
-        if received:
-            prev = ring[d, k + 1, far]
-            prev.wait_recv()
-            rows = zs.at[q, r : r + 256]
-            zs[q, r : r + 256] = (rows[...].astype(F32) + zr[d, slot - 1].astype(F32)).astype(BF16)
-        ring[d, k, far] = send(zs.at[q, pl.ds(r, 256)], zr.at[d, slot], at_z(BY[d]))
-
+        for i in range(2):
+            r = (FARZ if far else NEARZ)[d] + i * 128
+            rows = slice(r, r + 128)
+            if not first:
+                ring[d, k + 1, far, i].wait_recv()
+                came = zr[d, slot - 1, i * 128 : (i + 1) * 128]
+                zs[q, rows] = (zs[q, rows].astype(F32) + came.astype(F32)).astype(BF16)
+            ring[d, k, far, i] = send(zs.at[q, pl.ds(r, 128)], zr.at[d, slot, pl.ds(i * 128, 128)], at_z(BY[d]))
+
+    def z_both(k, far):
+        for d in range(2):
+            z_send(d, k, far)
+
+    pair_send(4)
+    pair_send(3)
+    pair_send(-3)
     pair_sum(4)
-    for d in range(2):
-        z_send(d, 4, True, False)
+    z_both(4, True)
     pair_sum(3)
     pair_sum(-3)
-    for d in range(2):
-        z_send(d, 3, False, False)
-    for k in order[3:]:
-        pair_sum(k)
-    for d in range(2):
-        z_send(d, 3, True, True)
-    grad_w(1, 0)
-    for k in (2, 1):
-        for far in (False, True):
-            for d in range(2):
-                z_send(d, k, far, True)
-        grad_w(1, 3 - k)
-    bo_last(0, bo_b0)
-    bo_last(1, bo_b1)
+    z_both(3, False)
+    pair_send(2)
+    pair_send(-2)
+    z_both(3, True)
+    pair_sum(2)
+    pair_sum(-2)
+    bo_a = bo_first()
+    pair_send(1)
+    pair_send(-1)
+    z_both(2, False)
+    pair_sum(1)
+    pair_sum(-1)
+    pair_send(0)
+    z_both(2, True)
+    grad_w(1, 0, 0)
+    grad_w(1, 0, 1)
+    z_both(1, False)
+    pair_sum(0)
+    bo_b = bo_second(bo_a)
+    grad_w(1, 1, 0)
+    z_both(1, True)
+    grad_w(1, 1, 1)
+    grad_w(1, 2, 0)
+    grad_w(1, 2, 1)
     for copy in sm_b:
         copy.wait_recv()
     for g in range(2):
@@ -429,10 +463,12 @@
     for d in range(1, 16):
         skips = skips + sm[d // 4, d % 4, 4:8, :]
     gs_out[...] = skips
-
-    for far, rows in ((False, 0), (True, 0)):
+    bo_last(bo_b)
+
+    for far in (False, True):
         for d in range(2):
-            ring[d, 1, far].wait_recv()
+            for i in range(2):
+                ring[d, 1, far, i].wait_recv()
     own = zs[z]
     top = own[:256].astype(F32) + zr[0, 3].astype(F32) + zr[1, 6].astype(F32)
     low = own[256:].astype(F32) + zr[1, 3].astype(F32) + zr[0, 6].astype(F32)
@@ -442,10 +478,20 @@
         copy.wait_send()
 
 
+def hand_on(*refs):
+    came, out, sems = refs[:5], refs[5:10], refs[10]
+    copies = [pltpu.make_async_copy(came[i], out[i], sems.at[i]) for i in range(5)]
+    for copy in copies:
+        copy.start()
+    for copy in copies:
+        copy.wait()
+
+
 def per_device(block_in, w_in, filt, skip, grad_y):
     tokens = block_in.shape[0]
     scale = tokens ** (-0.5)
     vmem = pl.BlockSpec(memory_space=pltpu.VMEM)
+    hbm = pl.BlockSpec(memory_space=pltpu.HBM)
     out_shape = (
         jax.ShapeDtypeStruct((128, 512), BF16),
         jax.ShapeDtypeStruct((128, 512), BF16),
@@ -454,6 +500,8 @@
         jax.ShapeDtypeStruct((4, 128), F32),
     )
     scratch = [
+        pltpu.VMEM((2048, 512), BF16),
+        pltpu.VMEM((3, 512, 512), BF16),
         pltpu.VMEM((3, 512, 512), BF16),
         pltpu.VMEM((512, 2048), BF16),
         pltpu.VMEM((2, 3, 4, 4, 16, 2048), BF16),
@@ -464,9 +512,9 @@
         pltpu.VMEM((4, 4, 2, 16, 128), BF16),
         pltpu.VMEM((4, 4, 2, 16, 128), BF16),
         pltpu.VMEM((4, 4, 2, 16, 128), BF16),
-        pltpu.VMEM((2, 4, 4, 16, 128), BF16),
-        pltpu.VMEM((2, 4, 4, 16, 128), BF16),
-        pltpu.VMEM((2, 4, 4, 16, 128), BF16),
+        pltpu.VMEM((4, 2, 4, 16, 128), BF16),
+        pltpu.VMEM((4, 2, 4, 16, 128), BF16),
+        pltpu.VMEM((4, 4, 2, 16, 128), BF16),
         pltpu.VMEM((4, 4, 8, 128), F32),
         pltpu.VMEM((8, 512, 128), BF16),
         pltpu.VMEM((8, 512, 128), BF16),
@@ -474,18 +522,27 @@
         pltpu.VMEM((2, 7, 256, 128), BF16),
         pltpu.SemaphoreType.DMA((N_SEMS,)),
         pltpu.SemaphoreType.DMA((N_SEMS,)),
+        pltpu.SemaphoreType.DMA((6,)),
     ]
-    block_out, grad_x, grad_w, grad_filt, grad_skip = pl.pallas_call(
+    results = pl.pallas_call(
         functools.partial(block_kernel, scale),
         out_shape=out_shape,
-        in_specs=[vmem] * 5,
+        in_specs=[hbm, hbm, vmem, vmem, vmem],
         out_specs=[vmem] * 5,
         scratch_shapes=scratch,
         compiler_params=pltpu.CompilerParams(
-            collective_id=0, has_side_effects=True, vmem_limit_bytes=60 * 2**20
+            collective_id=0, has_side_effects=True, vmem_limit_bytes=44 * 2**20
         ),
         cost_estimate=pl.CostEstimate(flops=10**10, bytes_accessed=10**7, transcendentals=0),
-    )(block_in, w_in, filt, skip.reshape(1, 512), grad_y)
+    )(*(pltpu.with_memory_space_constraint(a, pltpu.HBM) for a in (block_in, w_in, filt, skip.reshape(1, 512), grad_y)))
+    block_out, grad_x, grad_w, grad_filt, grad_skip = pl.pallas_call(
+        hand_on,
+        out_shape=out_shape,
+        in_specs=[vmem] * 5,
+        out_specs=[pl.BlockSpec(memory_space=pl.ANY)] * 5,
+        scratch_shapes=[pltpu.SemaphoreType.DMA((5,))],
+        compiler_params=pltpu.CompilerParams(vmem_limit_bytes=8 * 2**20),
+    )(*results)
     return block_out, grad_x, grad_w, grad_filt, grad_skip.reshape(512)
 
 

time: 116 us -> 106 us (0.914)
  local copies, waits for them, and re-layouts: 8.2 us -> 0 us
    unnamed x9 -> x0, local copies, waits for them, and re-layouts: 8.2 us -> none
    pallas_call x1, Pallas kernels: 105 us -> 102 us  [per_device(): pl.pallas_call(functools.partial(block_kernel, scale), out_shape=out_shap...]
    pallas_call x0 -> x1, Pallas kernels: none -> 1.8 us  [per_device(): pl.pallas_call(hand_on, out_shape=out_shape, in_specs=[vmem] * 5, out_spe...]
where the time goes in v2:
time: 106 us; the launch traced here: 105 us
  Pallas kernels  104 us (98%)
    pallas_call x1, Pallas kernels, per_device(): pl.pallas_call(functools.partial(block_kernel, scale), out_shape=out_shap...  102 us

profile of v2, /device:TPU:32, one launch (start us, length us, event | category | flops | bytes accessed | tf_op | source)
XLA Modules:
  0.0 104.9 jit_solution(6949112373347701368)
XLA Ops:
  0.6 102.3 %shard_map.92 = (bf16[128,512]{1,0:T(8,128)(2,1)S(1)}, bf16[128,512]{1,0:T(8,128)(2,1)S(1)}, f32[3,512,512]{2,1,0:T(8,128)S(1)}, f32[32,128]{1,0:T(8,128)S(1)}, f32[4,128]{1,0:T(4,128)S(1)}) custom-call(bf16[2048,512]{1,0:T(8,128)(2,1)} %bi_in.1, bf16[3,512,512]{2,1,0:T(8,128)(2,1)} %w_in.1, f32[32,128]{1,0:T(8,128)} %filt.1, f32[1,512]{1,0:T(1,128)} %bitcast.2, ...), custom_call_target="tpu_custom_call" | custom-call | flops 10000000000 | bytes 10000000 | tf_op jit(solution)/shard_map/pallas_call | solution.py:527
  102.9 1.8 %shard_map.93 = (bf16[128,512]{1,0:T(8,128)(2,1)}, bf16[128,512]{1,0:T(8,128)(2,1)}, f32[3,512,512]{2,1,0:T(8,128)}, f32[32,128]{1,0:T(8,128)}, f32[4,128]{1,0:T(4,128)}) custom-call(bf16[128,512]{1,0:T(8,128)(2,1)S(1)} %get-tuple-element.15.refs_0_, bf16[128,512]{1,0:T(8,128)(2,1)S(1)} %get-tuple-element.16.refs_1_, ...), custom_call_target="tpu_custom_call" | custom-call | tf_op jit(solution)/shard_map/pallas_call | solution.py:538

commit v3 on v2

--- a/solution.py
+++ b/solution.py
@@ -24,8 +24,8 @@
 
 
 def block_kernel(
-    scale, bi_in, w_in, filt, skip, gy, bo_out, gx_out, gw_out, gf_out, gs_out,
-    bi, w, wt, bit, part, r1, r2, gath, gx, gyt, gy1, gy2, bo0, bo1, bo2, sm, cs, cr, zs, zr, ssem, rsem, lsem,
+    scale, bi_in, w_in, filt_in, skip_in, gy_in, bo_out, gx_out, gw_out, gf_out, gs_out,
+    bi, w, filt, skip, gy, wt, bit, part, r1, r2, gath, gx, gyt, gy1, gy2, bo0, bo1, bo2, sm, cs, cr, zs, zr, ssem, rsem, lsem,
 ):
     seq, tp = lax.axis_index("seq"), lax.axis_index("tp")
     x, y, z, core = lax.rem(seq, 4), lax.div(seq, 4), lax.div(tp, 2), lax.rem(tp, 2)
@@ -59,6 +59,7 @@
 
     half_w = [pl.ds(0, 256), pl.ds(256, 256)]
     quarter = [pl.ds(i * QUARTER, QUARTER) for i in range(4)]
+    small_load = [load(gy_in, gy, 6), load(filt_in, filt, 7), load(skip_in, skip, 8)]
     w_load = [load(w_in.at[:, :, half_w[0]], w.at[:, :, half_w[0]], 0)]
     bi_load = [load(bi_in.at[q], bi.at[q], 2 + i) for i, q in enumerate(quarter)]
     w_load.append(load(w_in.at[:, :, half_w[1]], w.at[:, :, half_w[1]], 1))
@@ -324,16 +325,18 @@
             rows = jnp.concatenate([bo2[d % 4, d // 4, g] for d in range(16)], axis=0)
             bo_out[:, g * 256 : (g + 1) * 256] = rows.T
 
+    for copy in small_load:
+        copy.wait()
     gy_t = gy[...].T
     for g in range(2):
         for d in range(16):
             gyt[d % 4, d // 4, g] = gy_t[g * 256 + d * 16 : g * 256 + (d + 1) * 16]
     gy1[x] = gyt[x]
     sm[y, x] = jnp.zeros((8, 128), F32)
+    pl.semaphore_wait(barrier, len(partners))
+    gy_a = [send(gyt.at[m4(x + k)], gy1.at[x], at_x(k)) for k in (1, -1, 2)]
     w_load[0].wait()
     transpose_w(0)
-    pl.semaphore_wait(barrier, len(partners))
-    gy_a = [send(gyt.at[m4(x + k)], gy1.at[x], at_x(k)) for k in (1, -1, 2)]
     for i in range(4):
         bi_load[i].wait()
         project_rows(0, quarter[i])
@@ -376,17 +379,20 @@
     sm_a = [send(sm.at[y, x], sm.at[y, x], at_y(k)) for k in (1, -1, 2)]
     grad_x_near(0)
     grad_x_near(1)
+    grad_w(0, 0, 0)
+    grad_w(0, 0, 1)
     ag_forward(1, 1)
     ag_forward(1, 2)
+    grad_w(0, 1, 0)
+    grad_w(0, 1, 1)
     grad_x_near(2)
     grad_x_near(3)
+    grad_w(0, 2, 0)
+    grad_w(0, 2, 1)
     for copy in sm_a:
         copy.wait_recv()
     sm_b = [send(sm.at[:, x], sm.at[:, x], at_x(k)) for k in (1, -1, 2)]
     ag_forward(1, 3)
-    for j in range(3):
-        for i in range(2):
-            grad_w(0, j, i)
     ag_close(1)
 
     order = (4, 3, -3, 2, -2, 1, -1, 0)
@@ -425,12 +431,13 @@
 
     pair_send(4)
     pair_send(3)
-    pair_send(-3)
     pair_sum(4)
     z_both(4, True)
+    pair_send(-3)
     pair_sum(3)
+    z_send(0, 3, False)
     pair_sum(-3)
-    z_both(3, False)
+    z_send(1, 3, False)
     pair_send(2)
     pair_send(-2)
     z_both(3, True)
@@ -502,6 +509,9 @@
     scratch = [
         pltpu.VMEM((2048, 512), BF16),
         pltpu.VMEM((3, 512, 512), BF16),
+        pltpu.VMEM((32, 128), F32),
+        pltpu.VMEM((1, 512), F32),
+        pltpu.VMEM((128, 512), BF16),
         pltpu.VMEM((3, 512, 512), BF16),
         pltpu.VMEM((512, 2048), BF16),
         pltpu.VMEM((2, 3, 4, 4, 16, 2048), BF16),
@@ -522,12 +532,12 @@
         pltpu.VMEM((2, 7, 256, 128), BF16),
         pltpu.SemaphoreType.DMA((N_SEMS,)),
         pltpu.SemaphoreType.DMA((N_SEMS,)),
-        pltpu.SemaphoreType.DMA((6,)),
+        pltpu.SemaphoreType.DMA((9,)),
     ]
     results = pl.pallas_call(
         functools.partial(block_kernel, scale),
         out_shape=out_shape,
-        in_specs=[hbm, hbm, vmem, vmem, vmem],
+        in_specs=[hbm] * 5,
         out_specs=[vmem] * 5,
         scratch_shapes=scratch,
         compiler_params=pltpu.CompilerParams(

time: 106 us -> 105 us (level)
  no operation moved by 1% of the time
where the time goes in v3:
time: 105 us; the launch traced here: 104 us
  Pallas kernels  104 us (99%)
    pallas_call x1, Pallas kernels, per_device(): pl.pallas_call(functools.partial(block_kernel, scale), out_shape=out_shap...  102 us

profile of v3, /device:TPU:32, one launch (start us, length us, event | category | flops | bytes accessed | tf_op | source)
XLA Modules:
  0.0 104.4 jit_solution(6511967579724236086)
XLA Ops:
  0.6 101.8 %shard_map.92 = (bf16[128,512]{1,0:T(8,128)(2,1)S(1)}, bf16[128,512]{1,0:T(8,128)(2,1)S(1)}, f32[3,512,512]{2,1,0:T(8,128)S(1)}, f32[32,128]{1,0:T(8,128)S(1)}, f32[4,128]{1,0:T(4,128)S(1)}) custom-call(bf16[2048,512]{1,0:T(8,128)(2,1)} %bi_in.1, bf16[3,512,512]{2,1,0:T(8,128)(2,1)} %w_in.1, f32[32,128]{1,0:T(8,128)} %filt_in.1, f32[1,512]{1,0:T(1,128)} %bitcast.2, ...), custom_call_target="tpu_custom_call" | custom-call | flops 10000000000 | bytes 10000000 | tf_op jit(solution)/shard_map/pallas_call | solution.py:537
  102.4 1.8 %shard_map.93 = (bf16[128,512]{1,0:T(8,128)(2,1)}, bf16[128,512]{1,0:T(8,128)(2,1)}, f32[3,512,512]{2,1,0:T(8,128)}, f32[32,128]{1,0:T(8,128)}, f32[4,128]{1,0:T(4,128)}) custom-call(bf16[128,512]{1,0:T(8,128)(2,1)S(1)} %get-tuple-element.15.refs_0_, bf16[128,512]{1,0:T(8,128)(2,1)S(1)} %get-tuple-element.16.refs_1_, ...), custom_call_target="tpu_custom_call" | custom-call | tf_op jit(solution)/shard_map/pallas_call | solution.py:548

commit v4 on v3

--- a/solution.py
+++ b/solution.py
@@ -331,10 +331,12 @@
     for g in range(2):
         for d in range(16):
             gyt[d % 4, d // 4, g] = gy_t[g * 256 + d * 16 : g * 256 + (d + 1) * 16]
-    gy1[x] = gyt[x]
+    gy1[0, x] = gyt[x, :, 0]
+    gy1[1, y] = gyt[:, y, 1]
     sm[y, x] = jnp.zeros((8, 128), F32)
     pl.semaphore_wait(barrier, len(partners))
-    gy_a = [send(gyt.at[m4(x + k)], gy1.at[x], at_x(k)) for k in (1, -1, 2)]
+    gy_a = [send(gyt.at[m4(x + k), :, 0], gy1.at[0, x], at_x(k)) for k in (1, -1, 2)]
+    gy_a += [send(gyt.at[:, m4(y + k), 1], gy1.at[1, y], at_y(k)) for k in (1, -1, 2)]
     w_load[0].wait()
     transpose_w(0)
     for i in range(4):
@@ -346,8 +348,10 @@
     transpose_w(1)
     for copy in gy_a:
         copy.wait_recv()
-    gy2[y] = gy1[:, y]
-    gy_b = [send(gy1.at[:, m4(y + k)], gy2.at[y], at_y(k)) for k in (1, -1, 2)]
+    gy2[y, :, 0] = gy1[0, :, y]
+    gy2[:, x, 1] = gy1[1, :, x]
+    gy_b = [send(gy1.at[0, :, m4(y + k)], gy2.at[y, :, 0], at_y(k)) for k in (1, -1, 2)]
+    gy_b += [send(gy1.at[1, :, m4(x + k)], gy2.at[:, x, 1], at_x(k)) for k in (1, -1, 2)]
     project(1)
     send_s2b(0)
     send_s1(1)
@@ -520,7 +524,7 @@
         pltpu.VMEM((2, 3, 4, 4, 16, 2048), BF16),
         pltpu.VMEM((512, 2048), F32),
         pltpu.VMEM((4, 4, 2, 16, 128), BF16),
-        pltpu.VMEM((4, 4, 2, 16, 128), BF16),
+        pltpu.VMEM((2, 4, 4, 16, 128), BF16),
         pltpu.VMEM((4, 4, 2, 16, 128), BF16),
         pltpu.VMEM((4, 2, 4, 16, 128), BF16),
         pltpu.VMEM((4, 2, 4, 16, 128), BF16),

time: 105 us -> 105 us (level)
  no operation moved by 1% of the time
where the time goes in v4:
time: 105 us; the launch traced here: 104 us
  Pallas kernels  103 us (98%)
    pallas_call x1, Pallas kernels, per_device(): pl.pallas_call(functools.partial(block_kernel, scale), out_shape=out_shap...  101 us

profile of v4, /device:TPU:32, one launch (start us, length us, event | category | flops | bytes accessed | tf_op | source)
XLA Modules:
  0.0 103.7 jit_solution(8366501616789318130)
XLA Ops:
  0.6 101.1 %shard_map.92 = (bf16[128,512]{1,0:T(8,128)(2,1)S(1)}, bf16[128,512]{1,0:T(8,128)(2,1)S(1)}, f32[3,512,512]{2,1,0:T(8,128)S(1)}, f32[32,128]{1,0:T(8,128)S(1)}, f32[4,128]{1,0:T(4,128)S(1)}) custom-call(bf16[2048,512]{1,0:T(8,128)(2,1)} %bi_in.1, bf16[3,512,512]{2,1,0:T(8,128)(2,1)} %w_in.1, f32[32,128]{1,0:T(8,128)} %filt_in.1, f32[1,512]{1,0:T(1,128)} %bitcast.2, ...), custom_call_target="tpu_custom_call" | custom-call | flops 10000000000 | bytes 10000000 | tf_op jit(solution)/shard_map/pallas_call | solution.py:541
  101.8 1.8 %shard_map.93 = (bf16[128,512]{1,0:T(8,128)(2,1)}, bf16[128,512]{1,0:T(8,128)(2,1)}, f32[3,512,512]{2,1,0:T(8,128)}, f32[32,128]{1,0:T(8,128)}, f32[4,128]{1,0:T(4,128)}) custom-call(bf16[128,512]{1,0:T(8,128)(2,1)S(1)} %get-tuple-element.15.refs_0_, bf16[128,512]{1,0:T(8,128)(2,1)S(1)} %get-tuple-element.16.refs_1_, ...), custom_call_target="tpu_custom_call" | custom-call | tf_op jit(solution)/shard_map/pallas_call | solution.py:552
